TPU v7x, 256 devices: a whole 4x4x8 slice. The times are simulated.
256 devices in a mesh: light: 16 (over y, x), depth: 2 (over core), height: 8 (over z).
Axes of the slice: x: 4, y: 4, z: 8, core: 2. Of those that a mesh axis runs over, the one named last changes fastest.
Arguments:
- density: float32 [256, 32, 4096], P('light', 'depth', 'height'), may hold values from 0 to 6.4
- active_list: int32 [4, 384], P('depth'), may hold values from -1 to 511, as said below
- light_dir: int32 [8], replicated, may hold values from 0 to 1, as said below
- lamp_plane: float32 [8, 32, 4096], P(None, 'depth', 'height'), may hold values from 0.5 to 2
- extinction: float32 [8], replicated, may hold values from 0.00390625 to 0.01953125
- blur_weights: float32 [8, 25], replicated, may hold values from 0.2 to 16
- albedo: float32 [8], replicated, may hold values from 0.3 to 1
Outputs:
- rendered: float32 [8, 256, 4096], P('depth', 'light', 'height')
Inputs may be any that keep to these rules, and one draw needn't show every extreme that they name: `active_list`: each row lists distinct brick numbers lb * 32 + hb (lb the light slab of 16 slices, hb the height brick of 128 cells) of one depth slab of 8 cells, then -1 to its end; a row lists between 192 and 384 bricks, and some row lists 384. `light_dir`: exactly 4 entries are 1.
All inputs are finite; a program needn't handle non-finite values.
Results may differ from a plain program's by a relative error of at most 0.00016.
Values sent between devices are 32-bit elements; how exact they have to be, the bound alone decides.
A program may use at most 64 MiB of HBM per device.

v0:
```python
import jax
import jax.numpy as jnp
from jax import lax
from jax.experimental import pallas as pl
from jax.experimental.pallas import tpu as pltpu
from jax.sharding import PartitionSpec as P

MESH = pl.DeviceIdType.MESH
LOG2E = 1.4426950408889634
SLICES = 16
SLABS = 16
ROWS = 16
DEPTH = 32
WIDTH = 512
BLOCKS = WIDTH // 128
BRICK_ROWS = 8
EIGHTHS = 8
HALF = 4
BEFORE_MARCH = 2


def device(light, depth, height):
    return {"light": light, "depth": depth, "height": height}


def windows(block):
    lane = lax.broadcasted_iota(jnp.int32, (block.shape[0], 128), 1)
    parts = [block[:, 128 * m : 128 * m + 128] for m in range(BLOCKS)]
    near = [pltpu.roll(part, 32, 1) for part in parts]
    far = [pltpu.roll(part, 96, 1) for part in parts]
    made = [far[0]]
    for m in range(BLOCKS):
        made.append(near[m] if m == 0 else jnp.where(lane < 32, near[m - 1], near[m]))
        made.append(far[m] if m == BLOCKS - 1 else jnp.where(lane < 96, far[m], far[m + 1]))
    made.append(near[BLOCKS - 1])
    return made


def body(
    density, active, light_dir, lamp, extinction, blur_weights, albedo,
    out,
    dens, lampv, masked, wins, columns, edges, lampwin, lampbuf, lampedge, steps, leaving, planes, shade,
    load_sem, col_send, col_recv, up_send, down_send, edge_recv, mask_sem, lamp_sem, lampedge_sem, plane_sem,
):
    light, depth, height = (lax.axis_index(a) for a in ("light", "depth", "height"))
    heights = lax.axis_size("height")
    half, eighth = lax.div(light, EIGHTHS), lax.rem(light, EIGHTHS)
    sibling = 1 - depth
    has_below, has_above = height > 0, height < heights - 1
    low_edge = jnp.logical_and(eighth == 0, has_below)
    high_edge = jnp.logical_and(eighth == EIGHTHS - 1, has_above)
    mine = 2 * light + depth
    above, below = lax.rem(height + 1, heights), lax.rem(height + heights - 1, heights)
    first = HALF * half + 2 * depth

    chunk = SLICES // 4
    loads = [
        pltpu.make_async_copy(
            density.at[pl.ds(chunk * i, chunk)], dens.at[pl.ds(chunk * i, chunk)], load_sem.at[i]
        )
        for i in range(4)
    ]
    for load in loads:
        load.start()
    load_lamp = pltpu.make_async_copy(lamp.at[pl.ds(HALF * half, HALF)], lampv, load_sem.at[4])
    load_lamp.start()

    barrier = pltpu.get_barrier_semaphore()

    def greet(begin, at):
        @pl.loop(begin, 2 * SLABS)
        def _(j):
            other = lax.rem(mine + j, 2 * SLABS)
            pl.semaphore_signal(
                barrier,
                inc=1,
                device_id=device(lax.div(other, 2), lax.rem(other, 2), at),
                device_id_type=MESH,
            )

    greet(1, height)

    @pl.when(low_edge)
    def _():
        greet(0, below)

    @pl.when(high_edge)
    def _():
        greet(0, above)

    listed = active[...]
    live = []
    for m in range(BLOCKS):
        brick = light * (BLOCKS * heights) + height * BLOCKS + m
        found = jnp.max(jnp.where(listed == brick, 1.0, 0.0), axis=1, keepdims=True)
        live.append(
            jnp.concatenate(
                [jnp.broadcast_to(found[i : i + 1], (BRICK_ROWS, 128)) for i in range(2)], axis=0
            )
        )
    live = jnp.concatenate(live, axis=1)

    column = jnp.zeros((ROWS, WIDTH), jnp.float32)
    for i in range(4):
        loads[i].wait()
        for x in range(chunk * i, chunk * i + chunk):
            cells = dens[x] * live
            masked[depth, x] = cells
            column = column + cells
    for j, window in enumerate(windows(column)):
        wins[j] = window

    pl.semaphore_wait(
        barrier,
        2 * SLABS - 1 + 4 * has_below.astype(jnp.int32) + 4 * has_above.astype(jnp.int32),
    )

    @pl.loop(0, 2 * SLABS)
    def _(j):
        other = lax.rem(mine + j, 2 * SLABS)
        to = lax.div(other, 2)
        source = wins.at[lax.rem(to, EIGHTHS) + 1]

        @pl.when(j == 0)
        def _():
            pltpu.make_async_copy(source, columns.at[mine], col_recv).start()

        @pl.when(j > 0)
        def _():
            pltpu.make_async_remote_copy(
                source, columns.at[mine], col_send, col_recv,
                device_id=device(to, lax.rem(other, 2), height), device_id_type=MESH,
            ).start()

    @pl.when(has_above)
    def _():
        for j in range(4):
            pltpu.make_async_remote_copy(
                wins.at[EIGHTHS + 1], edges.at[mine], up_send, edge_recv,
                device_id=device(EIGHTHS * (j // 2), j % 2, above), device_id_type=MESH,
            ).start()

    @pl.when(has_below)
    def _():
        for j in range(4):
            pltpu.make_async_remote_copy(
                wins.at[0], edges.at[mine], down_send, edge_recv,
                device_id=device(EIGHTHS * (j // 2) + EIGHTHS - 1, j % 2, below), device_id_type=MESH,
            ).start()

    share = pltpu.make_async_remote_copy(
        masked.at[depth], masked.at[depth], mask_sem.at[0], mask_sem.at[1],
        device_id=device(light, sibling, height), device_id_type=MESH,
    )
    share.start()

    load_lamp.wait()
    for c in range(HALF):
        for j, window in enumerate(windows(lampv[c])):
            lampwin[j, c] = window
    share_lamp = pltpu.make_async_remote_copy(
        lampwin.at[eighth + 1, pl.ds(2 * sibling, 2)], lampbuf.at[depth], lamp_sem.at[0], lamp_sem.at[1],
        device_id=device(light, sibling, height), device_id_type=MESH,
    )
    share_lamp.start()
    lamp_up = jnp.logical_and(eighth == 0, has_above)
    lamp_down = jnp.logical_and(eighth == EIGHTHS - 1, has_below)

    def lamp_over(source, at):
        for to in range(2):
            pltpu.make_async_remote_copy(
                lampwin.at[source, pl.ds(2 * to, 2)], lampedge.at[depth], lampedge_sem.at[0], lampedge_sem.at[1],
                device_id=device(light, to, at), device_id_type=MESH,
            ).start()

    @pl.when(lamp_up)
    def _():
        lamp_over(EIGHTHS + 1, above)

    @pl.when(lamp_down)
    def _():
        lamp_over(0, below)

    lampbuf[depth] = lampwin[eighth + 1, pl.ds(2 * depth, 2)]

    lane = lax.broadcasted_iota(jnp.int32, (DEPTH, 128), 1)
    row = lax.broadcasted_iota(jnp.int32, (DEPTH, 128), 0)

    share.wait_recv()

    shown = [HALF * depth + i for i in range(HALF)]
    shown_down = [jnp.full((DEPTH, 128), light_dir[c], jnp.int32) == 1 for c in shown]
    shown_rate = [extinction[c] * -LOG2E for c in shown]

    def shading(m):
        lanes = pl.ds(pl.multiple_of(128 * m, 128), 128)

        def cells_of(x):
            return masked[:, x, :, lanes].reshape(DEPTH, 128)

        total = lax.fori_loop(
            0, SLICES, lambda x, t: t + cells_of(x), jnp.zeros((DEPTH, 128), jnp.float32), unroll=True
        )

        def one(x, running):
            cells = cells_of(x)
            after = running + cells
            behind = total - after
            optical = cells * (6.0 / DEPTH)
            summed = optical
            for step in (1, 2, 4, 8, 16):
                summed = summed + jnp.where(row >= step, pltpu.roll(summed, step, 0), 0.0)
            weight = jnp.exp(optical - summed) * (1.0 - jnp.exp(-optical))
            for i in range(HALF):
                before = jnp.where(shown_down[i], behind, running)
                shade[i, m, x] = jnp.exp2(before * shown_rate[i]) * weight
            return after

        def two(i, running):
            return one(2 * i + 1, one(2 * i, running))

        lax.fori_loop(0, SLICES // 2, two, jnp.zeros((DEPTH, 128), jnp.float32))

    @pl.loop(0, BEFORE_MARCH)
    def _(m):
        shading(m)

    pltpu.make_async_copy(columns, columns, col_recv).wait()
    share_lamp.wait_recv()

    @pl.when(jnp.logical_or(low_edge, high_edge))
    def _():
        pltpu.make_async_copy(edges, edges, edge_recv).wait()
        pltpu.make_async_copy(lampedge, lampedge, lampedge_sem.at[1]).wait()

    foreign = jnp.logical_or(
        lane < jnp.where(low_edge, 32, 0), lane >= jnp.where(high_edge, 96, 128)
    )
    inside = jnp.logical_and(
        lane >= jnp.where(jnp.logical_and(eighth == 0, height == 0), 32, 0),
        lane < jnp.where(jnp.logical_and(eighth == EIGHTHS - 1, height == heights - 1), 96, 128),
    )
    down = [jnp.full((DEPTH, 128), light_dir[first + i], jnp.int32) == 1 for i in range(2)]
    rate = [extinction[first + i] * -LOG2E for i in range(2)]
    scale = []
    for i in range(2):
        whole = blur_weights[first + i, 0]
        for t in range(1, 25):
            whole = whole + blur_weights[first + i, t]
        scale.append(jnp.where(inside, 1.0 / jnp.full((DEPTH, 128), whole, jnp.float32), 0.0))

    def column_of(k):
        own = columns[pl.ds(2 * k, 2)].reshape(DEPTH, 128)
        return jnp.where(foreign, edges[pl.ds(2 * k, 2)].reshape(DEPTH, 128), own)

    def factors(s):
        ahead, back = column_of(s), column_of(SLABS - 1 - s)
        return tuple(
            jnp.exp2(jnp.where(down[i], back, ahead) * rate[i]) * scale[i] for i in range(2)
        )

    def blurred(plane, i):
        moved = [plane if b == 0 else pltpu.roll(plane, (-b) % 128, 1) for b in range(-2, 3)]
        total = None
        for a in range(-2, 3):
            term = None
            for b in range(5):
                part = moved[b] * blur_weights[first + i, 5 * (a + 2) + b]
                term = part if term is None else term + part
            if a:
                term = pltpu.roll(term, (-a) % DEPTH, 0)
                term = jnp.where(row >= -a if a < 0 else row < DEPTH - a, term, 0.0)
            total = term if total is None else total + term
        return total

    def advance(s, carry):
        plane, factor = carry
        later = factors(s + 1)
        plane = tuple(blurred(plane[i] * factor[i], i) for i in range(2))
        for i in range(2):
            steps[i, s + 1] = plane[i]
        return plane, later

    start = []
    for i in range(2):
        own = jnp.concatenate([lampbuf[0, i], lampbuf[1, i]], axis=0)
        other = jnp.concatenate([lampedge[0, i], lampedge[1, i]], axis=0)
        start.append(jnp.where(foreign, other, own))
        steps[i, 0] = start[i]
    carry = lax.fori_loop(0, SLABS // 2 - 1, advance, (tuple(start), factors(0)))

    def send(k):
        alone = jnp.logical_and(k == light, half == depth)
        to = planes.at[depth * EIGHTHS + eighth]

        @pl.when(alone)
        def _():
            pltpu.make_async_copy(leaving.at[k], to, plane_sem.at[1]).start()

        @pl.when(jnp.logical_not(alone))
        def _():
            pltpu.make_async_remote_copy(
                leaving.at[k], to, plane_sem.at[0], plane_sem.at[1],
                device_id=device(k, half, height), device_id_type=MESH,
            ).start()

    def advance_and_send(j, carry):
        s = j + SLABS // 2 - 1
        carry = advance(s, carry)
        late = carry[0]
        early = [steps[i, SLABS - 2 - s] for i in range(2)]
        front = [jnp.where(down[i], early[i], late[i]) for i in range(2)]
        rear = [jnp.where(down[i], late[i], early[i]) for i in range(2)]
        for k, pair in ((s + 1, front), (SLABS - 2 - s, rear)):
            leaving[k] = jnp.where(lane < 64, pltpu.roll(pair[0], 96, 1), pltpu.roll(pair[1], 32, 1))
            send(k)
        return carry

    lax.fori_loop(0, SLABS // 2, advance_and_send, carry)

    @pl.loop(BEFORE_MARCH, BLOCKS)
    def _(m):
        shading(m)

    pltpu.make_async_copy(planes, planes, plane_sem.at[1]).wait()

    for m in range(BLOCKS):
        lanes = pl.ds(128 * m, 128)
        for pair in range(2):
            even, odd = planes[EIGHTHS * pair + 2 * m], planes[EIGHTHS * pair + 2 * m + 1]
            entering = (
                jnp.where(lane < 64, even, pltpu.roll(odd, 64, 1)),
                jnp.where(lane < 64, pltpu.roll(even, 64, 1), odd),
            )
            for i in range(2):
                c = 2 * pair + i
                seen = jnp.sum(shade[c, m] * entering[i][None], axis=1)
                out[c, :, lanes] = seen * albedo[HALF * depth + c]

    pltpu.make_async_copy(
        columns.at[pl.ds(0, 2 * SLABS - 1)], columns.at[pl.ds(0, 2 * SLABS - 1)], col_send
    ).wait()

    @pl.when(has_above)
    def _():
        pltpu.make_async_copy(wins.at[pl.ds(0, 4)], wins.at[pl.ds(0, 4)], up_send).wait()

    @pl.when(has_below)
    def _():
        pltpu.make_async_copy(wins.at[pl.ds(0, 4)], wins.at[pl.ds(0, 4)], down_send).wait()

    share.wait_send()
    share_lamp.wait_send()

    @pl.when(jnp.logical_or(lamp_up, lamp_down))
    def _():
        pltpu.make_async_copy(lampedge, lampedge, lampedge_sem.at[0]).wait()

    @pl.when(half == depth)
    def _():
        part = leaving.at[pl.ds(0, SLABS - 1)]
        pltpu.make_async_copy(part, part, plane_sem.at[0]).wait()

    @pl.when(half != depth)
    def _():
        pltpu.make_async_copy(leaving, leaving, plane_sem.at[0]).wait()


def local(density, active_list, light_dir, lamp_plane, extinction, blur_weights, albedo):
    f32 = jnp.float32
    vmem = pl.BlockSpec(memory_space=pltpu.VMEM)
    smem = pl.BlockSpec(memory_space=pltpu.SMEM)
    anywhere = pl.BlockSpec(memory_space=pl.ANY)
    dma = pltpu.SemaphoreType.DMA
    return pl.pallas_call(
        body,
        out_shape=jax.ShapeDtypeStruct((HALF, SLICES, WIDTH), f32),
        in_specs=[anywhere, vmem, smem, anywhere, smem, smem, smem],
        out_specs=vmem,
        scratch_shapes=[
            pltpu.VMEM((SLICES, ROWS, WIDTH), f32),
            pltpu.VMEM((HALF, ROWS, WIDTH), f32),
            pltpu.VMEM((2, SLICES, ROWS, WIDTH), f32),
            pltpu.VMEM((EIGHTHS + 2, ROWS, 128), f32),
            pltpu.VMEM((2 * SLABS, ROWS, 128), f32),
            pltpu.VMEM((2 * SLABS, ROWS, 128), f32),
            pltpu.VMEM((EIGHTHS + 2, HALF, ROWS, 128), f32),
            pltpu.VMEM((2, 2, ROWS, 128), f32),
            pltpu.VMEM((2, 2, ROWS, 128), f32),
            pltpu.VMEM((2, SLABS, DEPTH, 128), f32),
            pltpu.VMEM((SLABS, DEPTH, 128), f32),
            pltpu.VMEM((2 * EIGHTHS, DEPTH, 128), f32),
            pltpu.VMEM((HALF, BLOCKS, SLICES, DEPTH, 128), f32),
            dma((5,)), dma(()), dma(()), dma(()), dma(()), dma(()), dma((2,)), dma((2,)), dma((2,)), dma((2,)),
        ],
        compiler_params=pltpu.CompilerParams(
            collective_id=0, has_side_effects=True, vmem_limit_bytes=40 * 1024 * 1024
        ),
        name="march_and_shade",
    )(density, active_list, light_dir, lamp_plane, extinction, blur_weights, albedo)


def solution(mesh):
    in_specs = (
        P("light", "depth", "height"),
        P("depth", None),
        P(),
        P(None, "depth", "height"),
        P(),
        P(),
        P(),
    )
    out_specs = P("depth", "light", "height")
    return jax.shard_map(local, mesh=mesh, in_specs=in_specs, out_specs=out_specs, check_vma=False)
```

profile of v0, /device:TPU:1, one launch (start us, length us, event | category | flops | bytes accessed | tf_op | source)
XLA Modules:
  0.0 32.0 jit_solution(11079086789918284452)
XLA Ops:
  0.0 0.0 copy-start
  0.0 1.0 %copy-done = f32[16,16,512]{2,1,0:T(8,128)S(1)} copy-done((f32[16,16,512]{2,1,0:T(8,128)S(1)}, f32[16,16,512]{2,1,0:T(8,128)}, u32[]{:S(2)}) %copy-start) | copy-done | bytes 524312
  1.0 0.0 copy-start.1
  1.0 0.9 %copy-done.1 = f32[8,16,512]{2,1,0:T(8,128)S(1)} copy-done((f32[8,16,512]{2,1,0:T(8,128)S(1)}, f32[8,16,512]{2,1,0:T(8,128)}, u32[]{:S(2)}) %copy-start.1) | copy-done | bytes 262168
  2.0 0.0 copy-start.2
  2.0 0.7 %copy-done.2 = f32[8,25]{1,0:T(8,128)S(1)} copy-done((f32[8,25]{1,0:T(8,128)S(1)}, f32[8,25]{1,0:T(8,128)}, u32[]{:S(2)}) %copy-start.2) | copy-done | bytes 824
  2.7 0.0 copy-start.3
  2.7 0.7 %copy-done.3 = s32[2,384]{1,0:T(2,128)S(1)} copy-done((s32[2,384]{1,0:T(2,128)S(1)}, s32[2,384]{1,0:T(2,128)}, u32[]{:S(2)}) %copy-start.3) | copy-done | bytes 3096
  3.4 0.0 copy-start.4
  3.4 0.7 %copy-done.4 = s32[8]{0:T(128)S(1)} copy-done((s32[8]{0:T(128)S(1)}, s32[8]{0:T(128)}, u32[]{:S(2)}) %copy-start.4) | copy-done | bytes 56
  4.0 0.0 copy-start.5
  4.0 0.7 %copy-done.5 = f32[8]{0:T(128)S(1)} copy-done((f32[8]{0:T(128)S(1)}, f32[8]{0:T(128)}, u32[]{:S(2)}) %copy-start.5) | copy-done | bytes 56
  4.7 0.0 copy-start.6
  4.7 0.7 %copy-done.6 = f32[8]{0:T(128)S(1)} copy-done((f32[8]{0:T(128)S(1)}, f32[8]{0:T(128)}, u32[]{:S(2)}) %copy-start.6) | copy-done | bytes 56
  5.3 26.0 %march_and_shade.1 = f32[4,16,512]{2,1,0:T(8,128)S(1)} custom-call(f32[16,16,512]{2,1,0:T(8,128)S(1)} %copy-done, s32[2,384]{1,0:T(2,128)S(1)} %copy-done.3, s32[8]{0:T(128)S(1)} %copy-done.4, f32[8,16,512]{2,1,0:T(8,128)S(1)} %copy-done.1, f32[8]{0:T(128)S(1)} %copy-done.5, f32[8,25]{1,0:T(8,128)S(1)} %copy-done.2, f32[8]{0:T(128)S(1)} %copy-done.6), custom_call_target="tpu_custom_call" | custom-call | tf_op jit(solution)/shard_map/march_and_shade/pallas_call | solution.py:375
  31.4 0.7 %copy.9 = f32[4,16,512]{2,1,0:T(8,128)} copy(f32[4,16,512]{2,1,0:T(8,128)S(1)} %march_and_shade.1) | data formatting | bytes 262144
Async XLA Ops:
  0.0 1.0 %copy-start = (f32[16,16,512]{2,1,0:T(8,128)S(1)}, f32[16,16,512]{2,1,0:T(8,128)}, u32[]{:S(2)}) copy-start(f32[16,16,512]{2,1,0:T(8,128)} %density.1) | copy-start | bytes 1572868
  1.0 0.9 %copy-start.1 = (f32[8,16,512]{2,1,0:T(8,128)S(1)}, f32[8,16,512]{2,1,0:T(8,128)}, u32[]{:S(2)}) copy-start(f32[8,16,512]{2,1,0:T(8,128)} %lamp.1) | copy-start | bytes 786436
  2.0 0.7 %copy-start.2 = (f32[8,25]{1,0:T(8,128)S(1)}, f32[8,25]{1,0:T(8,128)}, u32[]{:S(2)}) copy-start(f32[8,25]{1,0:T(8,128)} %blur_weights.1) | copy-start | bytes 2404
  2.7 0.7 %copy-start.3 = (s32[2,384]{1,0:T(2,128)S(1)}, s32[2,384]{1,0:T(2,128)}, u32[]{:S(2)}) copy-start(s32[2,384]{1,0:T(2,128)} %active.1) | copy-start | bytes 9220
  3.4 0.7 %copy-start.4 = (s32[8]{0:T(128)S(1)}, s32[8]{0:T(128)}, u32[]{:S(2)}) copy-start(s32[8]{0:T(128)} %light_dir.1) | copy-start | bytes 100
  4.0 0.7 %copy-start.5 = (f32[8]{0:T(128)S(1)}, f32[8]{0:T(128)}, u32[]{:S(2)}) copy-start(f32[8]{0:T(128)} %extinction.1) | copy-start | bytes 100
  4.7 0.7 %copy-start.6 = (f32[8]{0:T(128)S(1)}, f32[8]{0:T(128)}, u32[]{:S(2)}) copy-start(f32[8]{0:T(128)} %albedo.1) | copy-start | bytes 100
where the time goes:
time: 32.3 us; the launch traced here: 32 us
  Pallas kernels  26 us (80%)
  local copies, waits for them, and re-layouts  5.98 us (19%)
    pallas_call x1, Pallas kernels, local(): pl.pallas_call(body, out_shape=jax.ShapeDtypeStruct((HALF, SLICES, WIDTH)...  26 us
    unnamed x15, local copies, waits for them, and re-layouts  5.98 us

commit v1 on v0

--- a/solution.py
+++ b/solution.py
@@ -37,9 +37,9 @@
 
 
 def body(
-    density, active, light_dir, lamp, extinction, blur_weights, albedo,
+    density, active_hbm, light_dir_hbm, lamp, extinction_hbm, blur_hbm, albedo_hbm,
     out,
-    dens, lampv, masked, wins, columns, edges, lampwin, lampbuf, lampedge, steps, leaving, planes, shade,
+    active, light_dir, extinction, blur_weights, albedo, dens, lampv, masked, wins, columns, edges, lampwin, lampbuf, lampedge, steps, leaving, planes, shade,
     load_sem, col_send, col_recv, up_send, down_send, edge_recv, mask_sem, lamp_sem, lampedge_sem, plane_sem,
 ):
     light, depth, height = (lax.axis_index(a) for a in ("light", "depth", "height"))
@@ -64,6 +64,16 @@
         load.start()
     load_lamp = pltpu.make_async_copy(lamp.at[pl.ds(HALF * half, HALF)], lampv, load_sem.at[4])
     load_lamp.start()
+    load_active = pltpu.make_async_copy(active_hbm, active, load_sem.at[5])
+    load_small = [
+        pltpu.make_async_copy(light_dir_hbm, light_dir, load_sem.at[6]),
+        pltpu.make_async_copy(extinction_hbm, extinction, load_sem.at[7]),
+        pltpu.make_async_copy(blur_hbm, blur_weights, load_sem.at[8]),
+        pltpu.make_async_copy(albedo_hbm, albedo, load_sem.at[9]),
+    ]
+    load_active.start()
+    for load in load_small:
+        load.start()
 
     barrier = pltpu.get_barrier_semaphore()
 
@@ -88,6 +98,7 @@
     def _():
         greet(0, above)
 
+    load_active.wait()
     listed = active[...]
     live = []
     for m in range(BLOCKS):
@@ -188,6 +199,8 @@
 
     share.wait_recv()
 
+    for load in load_small:
+        load.wait()
     shown = [HALF * depth + i for i in range(HALF)]
     shown_down = [jnp.full((DEPTH, 128), light_dir[c], jnp.int32) == 1 for c in shown]
     shown_rate = [extinction[c] * -LOG2E for c in shown]
@@ -369,15 +382,19 @@
 def local(density, active_list, light_dir, lamp_plane, extinction, blur_weights, albedo):
     f32 = jnp.float32
     vmem = pl.BlockSpec(memory_space=pltpu.VMEM)
-    smem = pl.BlockSpec(memory_space=pltpu.SMEM)
     anywhere = pl.BlockSpec(memory_space=pl.ANY)
     dma = pltpu.SemaphoreType.DMA
     return pl.pallas_call(
         body,
         out_shape=jax.ShapeDtypeStruct((HALF, SLICES, WIDTH), f32),
-        in_specs=[anywhere, vmem, smem, anywhere, smem, smem, smem],
+        in_specs=[anywhere] * 7,
         out_specs=vmem,
         scratch_shapes=[
+            pltpu.VMEM(active_list.shape, jnp.int32),
+            pltpu.SMEM(light_dir.shape, jnp.int32),
+            pltpu.SMEM(extinction.shape, f32),
+            pltpu.SMEM(blur_weights.shape, f32),
+            pltpu.SMEM(albedo.shape, f32),
             pltpu.VMEM((SLICES, ROWS, WIDTH), f32),
             pltpu.VMEM((HALF, ROWS, WIDTH), f32),
             pltpu.VMEM((2, SLICES, ROWS, WIDTH), f32),
@@ -391,10 +408,10 @@
             pltpu.VMEM((SLABS, DEPTH, 128), f32),
             pltpu.VMEM((2 * EIGHTHS, DEPTH, 128), f32),
             pltpu.VMEM((HALF, BLOCKS, SLICES, DEPTH, 128), f32),
-            dma((5,)), dma(()), dma(()), dma(()), dma(()), dma(()), dma((2,)), dma((2,)), dma((2,)), dma((2,)),
+            dma((10,)), dma(()), dma(()), dma(()), dma(()), dma(()), dma((2,)), dma((2,)), dma((2,)), dma((2,)),
         ],
         compiler_params=pltpu.CompilerParams(
-            collective_id=0, has_side_effects=True, vmem_limit_bytes=40 * 1024 * 1024
+            collective_id=0, has_side_effects=True, vmem_limit_bytes=63 * 1024 * 1024
         ),
         name="march_and_shade",
     )(density, active_list, light_dir, lamp_plane, extinction, blur_weights, albedo)

time: 32.3 us -> 26.9 us (0.83)
  local copies, waits for them, and re-layouts: 5.98 us -> 1.57 us
  Pallas kernels: 26 us -> 25.2 us
    unnamed x15 -> x1, local copies, waits for them, and re-layouts: 5.98 us -> 1.57 us
    pallas_call x1, Pallas kernels: 26 us -> 25.2 us  [local(): pl.pallas_call(body, out_shape=jax.ShapeDtypeStruct((HALF, SLICES, WIDTH)...]
where the time goes in v1:
time: 26.9 us; the launch traced here: 26.8 us
  Pallas kernels  25.2 us (94%)
  local copies, waits for them, and re-layouts  1.57 us (6%)
    pallas_call x1, Pallas kernels, local(): pl.pallas_call(body, out_shape=jax.ShapeDtypeStruct((HALF, SLICES, WIDTH)...  25.2 us
    unnamed x1, local copies, waits for them, and re-layouts  1.57 us

profile of v1, /device:TPU:1, one launch (start us, length us, event | category | flops | bytes accessed | tf_op | source)
XLA Modules:
  0.0 26.8 jit_solution(10558933638343072635)
XLA Ops:
  0.0 25.2 %march_and_shade.1 = f32[4,16,512]{2,1,0:T(8,128)} custom-call(f32[16,16,512]{2,1,0:T(8,128)} %density.1, s32[2,384]{1,0:T(2,128)} %active_hbm.1, s32[8]{0:T(128)} %light_dir_hbm.1, f32[8,16,512]{2,1,0:T(8,128)} %lamp.1, f32[8]{0:T(128)} %extinction_hbm.1, f32[8,25]{1,0:T(8,128)} %blur_hbm.1, f32[8]{0:T(128)} %albedo_hbm.1), custom_call_target="tpu_custom_call" | custom-call | tf_op jit(solution)/shard_map/march_and_shade/pallas_call | solution.py:387
  25.3 1.6 %copy.9 = f32[4,16,512]{2,1,0:T(8,128)} copy(f32[4,16,512]{2,1,0:T(8,128)} %march_and_shade.1) | data formatting | bytes 262144

commit v2 on v1

--- a/solution.py
+++ b/solution.py
@@ -16,7 +16,37 @@
 BRICK_ROWS = 8
 EIGHTHS = 8
 HALF = 4
+BEFORE_RELAY = 1
 BEFORE_MARCH = 2
+SIDE = 4
+
+
+def hops(down, right):
+    return min(down, SIDE - down) + min(right, SIDE - right)
+
+
+OTHERS = sorted(
+    ((down, right) for down in range(SIDE) for right in range(SIDE) if down or right),
+    key=lambda step: -hops(*step),
+)
+FAR = [step for step in OTHERS if hops(*step) > 2]
+NEAR = [step for step in OTHERS if hops(*step) <= 2]
+
+
+def chip_at(light, step):
+    down = lax.rem(lax.div(light, SIDE) + step[0], SIDE)
+    return SIDE * down + lax.rem(lax.rem(light, SIDE) + step[1], SIDE)
+
+
+def hops_between(one, other):
+    total = 0
+    for a, b in (
+        (lax.div(one, SIDE), lax.div(other, SIDE)),
+        (lax.rem(one, SIDE), lax.rem(other, SIDE)),
+    ):
+        way = lax.rem(a - b + SIDE, SIDE)
+        total = total + jnp.minimum(way, SIDE - way)
+    return total
 
 
 def device(light, depth, height):
@@ -36,11 +66,21 @@
     return made
 
 
+def packed_low(window):
+    lane = lax.broadcasted_iota(jnp.int32, (8, 128), 1)
+    return jnp.where(lane < 32, window[:8], pltpu.roll(window[8:], 32, 1))
+
+
+def packed_high(window):
+    lane = lax.broadcasted_iota(jnp.int32, (8, 128), 1)
+    return jnp.where(lane >= 96, window[:8], pltpu.roll(window[8:], 96, 1))
+
+
 def body(
     density, active_hbm, light_dir_hbm, lamp, extinction_hbm, blur_hbm, albedo_hbm,
     out,
-    active, light_dir, extinction, blur_weights, albedo, dens, lampv, masked, wins, columns, edges, lampwin, lampbuf, lampedge, steps, leaving, planes, shade,
-    load_sem, col_send, col_recv, up_send, down_send, edge_recv, mask_sem, lamp_sem, lampedge_sem, plane_sem,
+    active, light_dir, extinction, blur_weights, albedo, dens, lampv, masked, wins, rims, columns, packed, edges, lampwin, lamprim, lampbuf, lampedge, steps, leaving, planes, shade, taps,
+    load_sem, col_send, far_recv, near_recv, relay_sem, up_send, down_send, rim_recv, rim_sem, mask_sem, lamp_sem, lampedge_sem, plane_sem,
 ):
     light, depth, height = (lax.axis_index(a) for a in ("light", "depth", "height"))
     heights = lax.axis_size("height")
@@ -62,6 +102,34 @@
     ]
     for load in loads:
         load.start()
+    barrier = pltpu.get_barrier_semaphore()
+
+    def greet(to, core, at):
+        pl.semaphore_signal(barrier, inc=1, device_id=device(to, core, at), device_id_type=MESH)
+
+    def greet_group(at):
+        @pl.loop(0, 2 * SLABS)
+        def _(j):
+            other = lax.rem(mine + SLABS + j, 2 * SLABS)
+            greet(lax.div(other, 2), lax.rem(other, 2), at)
+
+    for step in FAR:
+        for core in range(2):
+            greet(chip_at(light, step), core, height)
+
+    @pl.when(low_edge)
+    def _():
+        greet_group(below)
+
+    @pl.when(high_edge)
+    def _():
+        greet_group(above)
+
+    for step in NEAR:
+        for core in range(2):
+            greet(chip_at(light, step), core, height)
+    greet(light, sibling, height)
+
     load_lamp = pltpu.make_async_copy(lamp.at[pl.ds(HALF * half, HALF)], lampv, load_sem.at[4])
     load_lamp.start()
     load_active = pltpu.make_async_copy(active_hbm, active, load_sem.at[5])
@@ -75,29 +143,6 @@
     for load in load_small:
         load.start()
 
-    barrier = pltpu.get_barrier_semaphore()
-
-    def greet(begin, at):
-        @pl.loop(begin, 2 * SLABS)
-        def _(j):
-            other = lax.rem(mine + j, 2 * SLABS)
-            pl.semaphore_signal(
-                barrier,
-                inc=1,
-                device_id=device(lax.div(other, 2), lax.rem(other, 2), at),
-                device_id_type=MESH,
-            )
-
-    greet(1, height)
-
-    @pl.when(low_edge)
-    def _():
-        greet(0, below)
-
-    @pl.when(high_edge)
-    def _():
-        greet(0, above)
-
     load_active.wait()
     listed = active[...]
     live = []
@@ -118,46 +163,53 @@
             cells = dens[x] * live
             masked[depth, x] = cells
             column = column + cells
-    for j, window in enumerate(windows(column)):
-        wins[j] = window
+    made = windows(column)
+    for j in range(EIGHTHS):
+        wins[j] = made[j + 1]
+    rims[0] = packed_high(made[0])
+    rims[1] = packed_low(made[-1])
 
     pl.semaphore_wait(
         barrier,
         2 * SLABS - 1 + 4 * has_below.astype(jnp.int32) + 4 * has_above.astype(jnp.int32),
     )
 
-    @pl.loop(0, 2 * SLABS)
-    def _(j):
-        other = lax.rem(mine + j, 2 * SLABS)
-        to = lax.div(other, 2)
-        source = wins.at[lax.rem(to, EIGHTHS) + 1]
-
-        @pl.when(j == 0)
-        def _():
-            pltpu.make_async_copy(source, columns.at[mine], col_recv).start()
-
-        @pl.when(j > 0)
-        def _():
-            pltpu.make_async_remote_copy(
-                source, columns.at[mine], col_send, col_recv,
-                device_id=device(to, lax.rem(other, 2), height), device_id_type=MESH,
-            ).start()
+    def send_rim(side, to, at, left):
+        pltpu.make_async_remote_copy(
+            rims.at[side], packed.at[depth, light], left, rim_recv,
+            device_id=device(to, depth, at), device_id_type=MESH,
+        ).start()
 
     @pl.when(has_above)
     def _():
-        for j in range(4):
-            pltpu.make_async_remote_copy(
-                wins.at[EIGHTHS + 1], edges.at[mine], up_send, edge_recv,
-                device_id=device(EIGHTHS * (j // 2), j % 2, above), device_id_type=MESH,
-            ).start()
+        for to in (0, EIGHTHS):
+            send_rim(1, to, above, up_send)
 
     @pl.when(has_below)
     def _():
-        for j in range(4):
-            pltpu.make_async_remote_copy(
-                wins.at[0], edges.at[mine], down_send, edge_recv,
-                device_id=device(EIGHTHS * (j // 2) + EIGHTHS - 1, j % 2, below), device_id_type=MESH,
-            ).start()
+        for to in (EIGHTHS - 1, SLABS - 1):
+            send_rim(0, to, below, down_send)
+
+    def send_window(to, core, arrived):
+        pltpu.make_async_remote_copy(
+            wins.at[lax.rem(to, EIGHTHS)], columns.at[mine], col_send, arrived,
+            device_id=device(to, core, height), device_id_type=MESH,
+        ).start()
+
+    for step in FAR:
+        for core in range(2):
+            send_window(chip_at(light, step), core, far_recv)
+    for step in NEAR:
+        send_window(chip_at(light, step), depth, near_recv)
+
+    def relay(block, source):
+        pltpu.make_async_remote_copy(
+            source, columns.at[block], relay_sem.at[0], relay_sem.at[1],
+            device_id=device(light, sibling, height), device_id_type=MESH,
+        ).start()
+
+    relay(mine, wins.at[eighth])
+    columns[mine] = wins[eighth]
 
     share = pltpu.make_async_remote_copy(
         masked.at[depth], masked.at[depth], mask_sem.at[0], mask_sem.at[1],
@@ -167,10 +219,13 @@
 
     load_lamp.wait()
     for c in range(HALF):
-        for j, window in enumerate(windows(lampv[c])):
-            lampwin[j, c] = window
+        made = windows(lampv[c])
+        for j in range(EIGHTHS):
+            lampwin[j, c] = made[j + 1]
+        lamprim[0, c] = packed_high(made[0])
+        lamprim[1, c] = packed_low(made[-1])
     share_lamp = pltpu.make_async_remote_copy(
-        lampwin.at[eighth + 1, pl.ds(2 * sibling, 2)], lampbuf.at[depth], lamp_sem.at[0], lamp_sem.at[1],
+        lampwin.at[eighth, pl.ds(2 * sibling, 2)], lampbuf.at[depth], lamp_sem.at[0], lamp_sem.at[1],
         device_id=device(light, sibling, height), device_id_type=MESH,
     )
     share_lamp.start()
@@ -180,19 +235,19 @@
     def lamp_over(source, at):
         for to in range(2):
             pltpu.make_async_remote_copy(
-                lampwin.at[source, pl.ds(2 * to, 2)], lampedge.at[depth], lampedge_sem.at[0], lampedge_sem.at[1],
+                lamprim.at[source, pl.ds(2 * to, 2)], lampedge.at[depth], lampedge_sem.at[0], lampedge_sem.at[1],
                 device_id=device(light, to, at), device_id_type=MESH,
             ).start()
 
     @pl.when(lamp_up)
     def _():
-        lamp_over(EIGHTHS + 1, above)
+        lamp_over(1, above)
 
     @pl.when(lamp_down)
     def _():
         lamp_over(0, below)
 
-    lampbuf[depth] = lampwin[eighth + 1, pl.ds(2 * depth, 2)]
+    lampbuf[depth] = lampwin[eighth, pl.ds(2 * depth, 2)]
 
     lane = lax.broadcasted_iota(jnp.int32, (DEPTH, 128), 1)
     row = lax.broadcasted_iota(jnp.int32, (DEPTH, 128), 0)
@@ -234,17 +289,56 @@
 
         lax.fori_loop(0, SLICES // 2, two, jnp.zeros((DEPTH, 128), jnp.float32))
 
-    @pl.loop(0, BEFORE_MARCH)
+    for i in range(2):
+        for t in range(25):
+            taps[i, t] = jnp.full((8, 128), blur_weights[first + i, t], jnp.float32)
+
+    @pl.loop(0, BEFORE_RELAY)
     def _(m):
         shading(m)
 
-    pltpu.make_async_copy(columns, columns, col_recv).wait()
+    pltpu.make_async_copy(
+        columns.at[pl.ds(0, len(NEAR))], columns.at[pl.ds(0, len(NEAR))], near_recv
+    ).wait()
+    for step in NEAR:
+        block = 2 * chip_at(light, step) + depth
+        relay(block, columns.at[block])
+    share_rims = pltpu.make_async_remote_copy(
+        packed.at[depth], packed.at[depth], rim_sem.at[0], rim_sem.at[1],
+        device_id=device(light, sibling, height), device_id_type=MESH,
+    )
+    on_edge = jnp.logical_or(low_edge, high_edge)
+
+    @pl.when(on_edge)
+    def _():
+        pltpu.make_async_copy(packed.at[0], packed.at[0], rim_recv).wait()
+        share_rims.start()
+
+    @pl.loop(BEFORE_RELAY, BEFORE_MARCH)
+    def _(m):
+        shading(m)
+
+    pltpu.make_async_copy(
+        columns.at[pl.ds(0, 2 * len(FAR))], columns.at[pl.ds(0, 2 * len(FAR))], far_recv
+    ).wait()
+    pltpu.make_async_copy(
+        columns.at[pl.ds(0, len(NEAR) + 1)], columns.at[pl.ds(0, len(NEAR) + 1)], relay_sem.at[1]
+    ).wait()
     share_lamp.wait_recv()
 
-    @pl.when(jnp.logical_or(low_edge, high_edge))
-    def _():
-        pltpu.make_async_copy(edges, edges, edge_recv).wait()
+    def unpacked(rim):
+        turned = jnp.where(eighth == 0, pltpu.roll(rim, 96, 1), pltpu.roll(rim, 32, 1))
+        return jnp.concatenate([rim, turned], axis=0)
+
+    @pl.when(on_edge)
+    def _():
+        share_rims.wait_recv()
         pltpu.make_async_copy(lampedge, lampedge, lampedge_sem.at[1]).wait()
+
+        @pl.loop(0, SLABS)
+        def _(k):
+            for z in range(2):
+                edges[2 * k + z] = unpacked(packed[z, k])
 
     foreign = jnp.logical_or(
         lane < jnp.where(low_edge, 32, 0), lane >= jnp.where(high_edge, 96, 128)
@@ -278,7 +372,7 @@
         for a in range(-2, 3):
             term = None
             for b in range(5):
-                part = moved[b] * blur_weights[first + i, 5 * (a + 2) + b]
+                part = (moved[b].reshape(DEPTH // 8, 8, 128) * taps[i, 5 * (a + 2) + b][None]).reshape(DEPTH, 128)
                 term = part if term is None else term + part
             if a:
                 term = pltpu.roll(term, (-a) % DEPTH, 0)
@@ -297,7 +391,7 @@
     start = []
     for i in range(2):
         own = jnp.concatenate([lampbuf[0, i], lampbuf[1, i]], axis=0)
-        other = jnp.concatenate([lampedge[0, i], lampedge[1, i]], axis=0)
+        other = jnp.concatenate([unpacked(lampedge[0, i]), unpacked(lampedge[1, i])], axis=0)
         start.append(jnp.where(foreign, other, own))
         steps[i, 0] = start[i]
     carry = lax.fori_loop(0, SLABS // 2 - 1, advance, (tuple(start), factors(0)))
@@ -327,6 +421,7 @@
         for k, pair in ((s + 1, front), (SLABS - 2 - s, rear)):
             leaving[k] = jnp.where(lane < 64, pltpu.roll(pair[0], 96, 1), pltpu.roll(pair[1], 32, 1))
             send(k)
+
         return carry
 
     lax.fori_loop(0, SLABS // 2, advance_and_send, carry)
@@ -351,16 +446,23 @@
                 out[c, :, lanes] = seen * albedo[HALF * depth + c]
 
     pltpu.make_async_copy(
-        columns.at[pl.ds(0, 2 * SLABS - 1)], columns.at[pl.ds(0, 2 * SLABS - 1)], col_send
+        columns.at[pl.ds(0, len(NEAR) + 2 * len(FAR))], columns.at[pl.ds(0, len(NEAR) + 2 * len(FAR))], col_send
     ).wait()
+    pltpu.make_async_copy(
+        columns.at[pl.ds(0, len(NEAR) + 1)], columns.at[pl.ds(0, len(NEAR) + 1)], relay_sem.at[0]
+    ).wait()
 
     @pl.when(has_above)
     def _():
-        pltpu.make_async_copy(wins.at[pl.ds(0, 4)], wins.at[pl.ds(0, 4)], up_send).wait()
+        pltpu.make_async_copy(rims, rims, up_send).wait()
 
     @pl.when(has_below)
     def _():
-        pltpu.make_async_copy(wins.at[pl.ds(0, 4)], wins.at[pl.ds(0, 4)], down_send).wait()
+        pltpu.make_async_copy(rims, rims, down_send).wait()
+
+    @pl.when(on_edge)
+    def _():
+        share_rims.wait_send()
 
     share.wait_send()
     share_lamp.wait_send()
@@ -398,17 +500,21 @@
             pltpu.VMEM((SLICES, ROWS, WIDTH), f32),
             pltpu.VMEM((HALF, ROWS, WIDTH), f32),
             pltpu.VMEM((2, SLICES, ROWS, WIDTH), f32),
-            pltpu.VMEM((EIGHTHS + 2, ROWS, 128), f32),
+            pltpu.VMEM((EIGHTHS, ROWS, 128), f32),
+            pltpu.VMEM((2, 8, 128), f32),
             pltpu.VMEM((2 * SLABS, ROWS, 128), f32),
+            pltpu.VMEM((2, SLABS, 8, 128), f32),
             pltpu.VMEM((2 * SLABS, ROWS, 128), f32),
-            pltpu.VMEM((EIGHTHS + 2, HALF, ROWS, 128), f32),
+            pltpu.VMEM((EIGHTHS, HALF, ROWS, 128), f32),
+            pltpu.VMEM((2, HALF, 8, 128), f32),
             pltpu.VMEM((2, 2, ROWS, 128), f32),
-            pltpu.VMEM((2, 2, ROWS, 128), f32),
+            pltpu.VMEM((2, 2, 8, 128), f32),
             pltpu.VMEM((2, SLABS, DEPTH, 128), f32),
             pltpu.VMEM((SLABS, DEPTH, 128), f32),
             pltpu.VMEM((2 * EIGHTHS, DEPTH, 128), f32),
             pltpu.VMEM((HALF, BLOCKS, SLICES, DEPTH, 128), f32),
-            dma((10,)), dma(()), dma(()), dma(()), dma(()), dma(()), dma((2,)), dma((2,)), dma((2,)), dma((2,)),
+            pltpu.VMEM((2, 25, 8, 128), f32),
+            dma((10,)), dma(()), dma(()), dma(()), dma((2,)), dma(()), dma(()), dma(()), dma((2,)), dma((2,)), dma((2,)), dma((2,)), dma((2,)),
         ],
         compiler_params=pltpu.CompilerParams(
             collective_id=0, has_side_effects=True, vmem_limit_bytes=63 * 1024 * 1024

time: 26.9 us -> 25.5 us (0.948)
  the two profiles are of different devices: /device:TPU:1 before, /device:TPU:99 now
where the time goes in v2:
time: 25.5 us; the launch traced here: 25.4 us
  Pallas kernels  23.9 us (94%)
  local copies, waits for them, and re-layouts  1.57 us (6%)
    pallas_call x1, Pallas kernels, local(): pl.pallas_call(body, out_shape=jax.ShapeDtypeStruct((HALF, SLICES, WIDTH)...  23.9 us
    unnamed x1, local copies, waits for them, and re-layouts  1.57 us

profile of v2, /device:TPU:99, one launch (start us, length us, event | category | flops | bytes accessed | tf_op | source)
XLA Modules:
  0.0 25.4 jit_solution(14105643836110181171)
XLA Ops:
  0.0 23.9 %march_and_shade.1 = f32[4,16,512]{2,1,0:T(8,128)} custom-call(f32[16,16,512]{2,1,0:T(8,128)} %density.1, s32[2,384]{1,0:T(2,128)} %active_hbm.1, s32[8]{0:T(128)} %light_dir_hbm.1, f32[8,16,512]{2,1,0:T(8,128)} %lamp.1, f32[8]{0:T(128)} %extinction_hbm.1, f32[8,25]{1,0:T(8,128)} %blur_hbm.1, f32[8]{0:T(128)} %albedo_hbm.1), custom_call_target="tpu_custom_call" | custom-call | tf_op jit(solution)/shard_map/march_and_shade/pallas_call | solution.py:489
  23.9 1.6 %copy.9 = f32[4,16,512]{2,1,0:T(8,128)} copy(f32[4,16,512]{2,1,0:T(8,128)} %march_and_shade.1) | data formatting | bytes 262144

commit v3 on v2

--- a/solution.py
+++ b/solution.py
@@ -38,11 +38,19 @@
     return SIDE * down + lax.rem(lax.rem(light, SIDE) + step[1], SIDE)
 
 
+def half_of(light):
+    return 1 - light // EIGHTHS
+
+
+def eighth_of(light):
+    return (light % EIGHTHS // SIDE) * SIDE + (light + 3) % SIDE
+
+
 def hops_between(one, other):
     total = 0
     for a, b in (
-        (lax.div(one, SIDE), lax.div(other, SIDE)),
-        (lax.rem(one, SIDE), lax.rem(other, SIDE)),
+        (one // SIDE, other // SIDE),
+        (one % SIDE, other % SIDE),
     ):
         way = lax.rem(a - b + SIDE, SIDE)
         total = total + jnp.minimum(way, SIDE - way)
@@ -76,15 +84,19 @@
     return jnp.where(lane >= 96, window[:8], pltpu.roll(window[8:], 96, 1))
 
 
+def spread(rim, turn):
+    return jnp.concatenate([rim, pltpu.roll(rim, turn, 1)], axis=0)
+
+
 def body(
     density, active_hbm, light_dir_hbm, lamp, extinction_hbm, blur_hbm, albedo_hbm,
     out,
-    active, light_dir, extinction, blur_weights, albedo, dens, lampv, masked, wins, rims, columns, packed, edges, lampwin, lamprim, lampbuf, lampedge, steps, leaving, planes, shade, taps,
-    load_sem, col_send, far_recv, near_recv, relay_sem, up_send, down_send, rim_recv, rim_sem, mask_sem, lamp_sem, lampedge_sem, plane_sem,
+    active, light_dir, extinction, blur_weights, albedo, dens, lampv, masked, wins, rims, rims_in, columns, lampwin, lamprim, lampbuf, lampedge, steps, leaving, planes, shade, taps, lifted, image,
+    load_sem, col_send, late_send, far_recv, near_recv, relay_sem, up_sem, down_sem, mask_sem, lamp_sem, lampedge_sem, plane_send, plane_recv, out_sem,
 ):
     light, depth, height = (lax.axis_index(a) for a in ("light", "depth", "height"))
     heights = lax.axis_size("height")
-    half, eighth = lax.div(light, EIGHTHS), lax.rem(light, EIGHTHS)
+    half, eighth = half_of(light), eighth_of(light)
     sibling = 1 - depth
     has_below, has_above = height > 0, height < heights - 1
     low_edge = jnp.logical_and(eighth == 0, has_below)
@@ -107,23 +119,25 @@
     def greet(to, core, at):
         pl.semaphore_signal(barrier, inc=1, device_id=device(to, core, at), device_id_type=MESH)
 
-    def greet_group(at):
-        @pl.loop(0, 2 * SLABS)
-        def _(j):
-            other = lax.rem(mine + SLABS + j, 2 * SLABS)
-            greet(lax.div(other, 2), lax.rem(other, 2), at)
-
     for step in FAR:
         for core in range(2):
             greet(chip_at(light, step), core, height)
 
+    @pl.when(has_below)
+    def _():
+        greet(light, depth, below)
+
+    @pl.when(has_above)
+    def _():
+        greet(light, depth, above)
+
     @pl.when(low_edge)
     def _():
-        greet_group(below)
+        greet(light, sibling, below)
 
     @pl.when(high_edge)
     def _():
-        greet_group(above)
+        greet(light, sibling, above)
 
     for step in NEAR:
         for core in range(2):
@@ -169,47 +183,54 @@
     rims[0] = packed_high(made[0])
     rims[1] = packed_low(made[-1])
 
-    pl.semaphore_wait(
-        barrier,
-        2 * SLABS - 1 + 4 * has_below.astype(jnp.int32) + 4 * has_above.astype(jnp.int32),
+    lamp_up = jnp.logical_and(eighth == 0, has_above)
+    lamp_down = jnp.logical_and(eighth == EIGHTHS - 1, has_below)
+    reached = [flag.astype(jnp.int32) for flag in (has_below, has_above, lamp_down, lamp_up)]
+    pl.semaphore_wait(barrier, 2 * SLABS - 1 + sum(reached))
+
+    rim_up = pltpu.make_async_remote_copy(
+        rims.at[1], rims_in.at[1], up_sem.at[0], up_sem.at[1],
+        device_id=device(light, depth, above), device_id_type=MESH,
     )
-
-    def send_rim(side, to, at, left):
+    rim_down = pltpu.make_async_remote_copy(
+        rims.at[0], rims_in.at[0], down_sem.at[0], down_sem.at[1],
+        device_id=device(light, depth, below), device_id_type=MESH,
+    )
+
+    @pl.when(has_above)
+    def _():
+        rim_up.start()
+
+    @pl.when(has_below)
+    def _():
+        rim_down.start()
+
+    def send_window(to, core, arrived, left=col_send):
         pltpu.make_async_remote_copy(
-            rims.at[side], packed.at[depth, light], left, rim_recv,
-            device_id=device(to, depth, at), device_id_type=MESH,
-        ).start()
-
-    @pl.when(has_above)
-    def _():
-        for to in (0, EIGHTHS):
-            send_rim(1, to, above, up_send)
-
-    @pl.when(has_below)
-    def _():
-        for to in (EIGHTHS - 1, SLABS - 1):
-            send_rim(0, to, below, down_send)
-
-    def send_window(to, core, arrived):
-        pltpu.make_async_remote_copy(
-            wins.at[lax.rem(to, EIGHTHS)], columns.at[mine], col_send, arrived,
+            wins.at[eighth_of(to)], columns.at[mine], left, arrived,
             device_id=device(to, core, height), device_id_type=MESH,
         ).start()
 
+    def at_rim(to):
+        return jnp.logical_or(eighth_of(to) == 0, eighth_of(to) == EIGHTHS - 1)
+
+    def send_far(to):
+        for core in range(2):
+            send_window(to, core, far_recv)
+
     for step in FAR:
-        for core in range(2):
-            send_window(chip_at(light, step), core, far_recv)
+        to = chip_at(light, step)
+
+        @pl.when(jnp.logical_not(at_rim(to)))
+        def _():
+            send_far(to)
+
     for step in NEAR:
-        send_window(chip_at(light, step), depth, near_recv)
-
-    def relay(block, source):
-        pltpu.make_async_remote_copy(
-            source, columns.at[block], relay_sem.at[0], relay_sem.at[1],
-            device_id=device(light, sibling, height), device_id_type=MESH,
-        ).start()
-
-    relay(mine, wins.at[eighth])
-    columns[mine] = wins[eighth]
+        to = chip_at(light, step)
+
+        @pl.when(jnp.logical_not(at_rim(to)))
+        def _():
+            send_window(to, depth, near_recv)
 
     share = pltpu.make_async_remote_copy(
         masked.at[depth], masked.at[depth], mask_sem.at[0], mask_sem.at[1],
@@ -229,8 +250,6 @@
         device_id=device(light, sibling, height), device_id_type=MESH,
     )
     share_lamp.start()
-    lamp_up = jnp.logical_and(eighth == 0, has_above)
-    lamp_down = jnp.logical_and(eighth == EIGHTHS - 1, has_below)
 
     def lamp_over(source, at):
         for to in range(2):
@@ -248,6 +267,40 @@
         lamp_over(0, below)
 
     lampbuf[depth] = lampwin[eighth, pl.ds(2 * depth, 2)]
+
+    thin = lax.broadcasted_iota(jnp.int32, (ROWS, 128), 1)
+
+    @pl.when(has_below)
+    def _():
+        rim_up.wait_recv()
+        wins[0] = jnp.where(thin < 32, spread(rims_in[1], 96), wins[0])
+
+    @pl.when(has_above)
+    def _():
+        rim_down.wait_recv()
+        wins[EIGHTHS - 1] = jnp.where(thin >= 96, spread(rims_in[0], 32), wins[EIGHTHS - 1])
+
+    ends = [to for to in range(SLABS) if eighth_of(to) in (0, EIGHTHS - 1)]
+    for to in ends:
+        away = hops_between(to, light)
+
+        @pl.when(away > 2)
+        def _():
+            send_far(to)
+
+        @pl.when(jnp.logical_and(away > 0, away <= 2))
+        def _():
+            send_window(to, depth, near_recv)
+            send_window(to, sibling, near_recv, late_send.at[ends.index(to)])
+
+    def relay(block, source):
+        pltpu.make_async_remote_copy(
+            source, columns.at[block], relay_sem.at[0], relay_sem.at[1],
+            device_id=device(light, sibling, height), device_id_type=MESH,
+        ).start()
+
+    relay(mine, wins.at[eighth])
+    columns[mine] = wins[eighth]
 
     lane = lax.broadcasted_iota(jnp.int32, (DEPTH, 128), 1)
     row = lax.broadcasted_iota(jnp.int32, (DEPTH, 128), 0)
@@ -297,48 +350,16 @@
     def _(m):
         shading(m)
 
-    pltpu.make_async_copy(
-        columns.at[pl.ds(0, len(NEAR))], columns.at[pl.ds(0, len(NEAR))], near_recv
-    ).wait()
-    for step in NEAR:
-        block = 2 * chip_at(light, step) + depth
-        relay(block, columns.at[block])
-    share_rims = pltpu.make_async_remote_copy(
-        packed.at[depth], packed.at[depth], rim_sem.at[0], rim_sem.at[1],
-        device_id=device(light, sibling, height), device_id_type=MESH,
-    )
+    share_lamp.wait_recv()
+
     on_edge = jnp.logical_or(low_edge, high_edge)
 
     @pl.when(on_edge)
     def _():
-        pltpu.make_async_copy(packed.at[0], packed.at[0], rim_recv).wait()
-        share_rims.start()
-
-    @pl.loop(BEFORE_RELAY, BEFORE_MARCH)
-    def _(m):
-        shading(m)
-
-    pltpu.make_async_copy(
-        columns.at[pl.ds(0, 2 * len(FAR))], columns.at[pl.ds(0, 2 * len(FAR))], far_recv
-    ).wait()
-    pltpu.make_async_copy(
-        columns.at[pl.ds(0, len(NEAR) + 1)], columns.at[pl.ds(0, len(NEAR) + 1)], relay_sem.at[1]
-    ).wait()
-    share_lamp.wait_recv()
+        pltpu.make_async_copy(lampedge, lampedge, lampedge_sem.at[1]).wait()
 
     def unpacked(rim):
-        turned = jnp.where(eighth == 0, pltpu.roll(rim, 96, 1), pltpu.roll(rim, 32, 1))
-        return jnp.concatenate([rim, turned], axis=0)
-
-    @pl.when(on_edge)
-    def _():
-        share_rims.wait_recv()
-        pltpu.make_async_copy(lampedge, lampedge, lampedge_sem.at[1]).wait()
-
-        @pl.loop(0, SLABS)
-        def _(k):
-            for z in range(2):
-                edges[2 * k + z] = unpacked(packed[z, k])
+        return jnp.where(jnp.broadcast_to(eighth == 0, (ROWS, 128)), spread(rim, 96), spread(rim, 32))
 
     foreign = jnp.logical_or(
         lane < jnp.where(low_edge, 32, 0), lane >= jnp.where(high_edge, 96, 128)
@@ -356,9 +377,44 @@
             whole = whole + blur_weights[first + i, t]
         scale.append(jnp.where(inside, 1.0 / jnp.full((DEPTH, 128), whole, jnp.float32), 0.0))
 
+    for i in range(2):
+        lifted[i] = jnp.zeros((DEPTH + 16, 128), jnp.float32)
+
+    start = []
+    for i in range(2):
+        own = jnp.concatenate([lampbuf[0, i], lampbuf[1, i]], axis=0)
+        other = jnp.concatenate([unpacked(lampedge[0, i]), unpacked(lampedge[1, i])], axis=0)
+        start.append(jnp.where(foreign, other, own))
+        steps[i, 0] = start[i]
+    def wait_blocks(count, semaphore):
+        some = columns.at[pl.ds(0, count)]
+        pltpu.make_async_copy(some, some, semaphore).wait()
+
+    late = at_rim(light)
+
+    @pl.when(jnp.logical_not(late))
+    def _():
+        wait_blocks(len(NEAR), near_recv)
+        for step in NEAR:
+            block = 2 * chip_at(light, step) + depth
+            relay(block, columns.at[block])
+
+    @pl.loop(BEFORE_RELAY, BEFORE_MARCH)
+    def _(m):
+        shading(m)
+
+    @pl.when(late)
+    def _():
+        wait_blocks(2 * len(NEAR), near_recv)
+        wait_blocks(1, relay_sem.at[1])
+
+    @pl.when(jnp.logical_not(late))
+    def _():
+        wait_blocks(len(NEAR) + 1, relay_sem.at[1])
+
+    wait_blocks(2 * len(FAR), far_recv)
     def column_of(k):
-        own = columns[pl.ds(2 * k, 2)].reshape(DEPTH, 128)
-        return jnp.where(foreign, edges[pl.ds(2 * k, 2)].reshape(DEPTH, 128), own)
+        return columns[pl.ds(2 * k, 2)].reshape(DEPTH, 128)
 
     def factors(s):
         ahead, back = column_of(s), column_of(SLABS - 1 - s)
@@ -367,16 +423,20 @@
         )
 
     def blurred(plane, i):
-        moved = [plane if b == 0 else pltpu.roll(plane, (-b) % 128, 1) for b in range(-2, 3)]
+        lifted[i, 8 : 8 + DEPTH] = plane
+        moved = [
+            plane if a == 0 else lifted[i, 8 + a : 8 + a + DEPTH] for a in range(-2, 3)
+        ]
+        moved = [part.reshape(DEPTH // 8, 8, 128) for part in moved]
         total = None
-        for a in range(-2, 3):
+        for b in range(-2, 3):
             term = None
-            for b in range(5):
-                part = (moved[b].reshape(DEPTH // 8, 8, 128) * taps[i, 5 * (a + 2) + b][None]).reshape(DEPTH, 128)
+            for a in range(5):
+                part = moved[a] * taps[i, 5 * a + b + 2][None]
                 term = part if term is None else term + part
-            if a:
-                term = pltpu.roll(term, (-a) % DEPTH, 0)
-                term = jnp.where(row >= -a if a < 0 else row < DEPTH - a, term, 0.0)
+            term = term.reshape(DEPTH, 128)
+            if b:
+                term = pltpu.roll(term, (-b) % 128, 1)
             total = term if total is None else total + term
         return total
 
@@ -388,26 +448,17 @@
             steps[i, s + 1] = plane[i]
         return plane, later
 
-    start = []
-    for i in range(2):
-        own = jnp.concatenate([lampbuf[0, i], lampbuf[1, i]], axis=0)
-        other = jnp.concatenate([unpacked(lampedge[0, i]), unpacked(lampedge[1, i])], axis=0)
-        start.append(jnp.where(foreign, other, own))
-        steps[i, 0] = start[i]
     carry = lax.fori_loop(0, SLABS // 2 - 1, advance, (tuple(start), factors(0)))
 
+    own_part = half == depth
+    arrived = plane_recv.at[lax.div(eighth, 2)]
+    place = planes.at[lax.div(eighth, 2), 2 * lax.rem(eighth, 2) + depth]
+
     def send(k):
-        alone = jnp.logical_and(k == light, half == depth)
-        to = planes.at[depth * EIGHTHS + eighth]
-
-        @pl.when(alone)
-        def _():
-            pltpu.make_async_copy(leaving.at[k], to, plane_sem.at[1]).start()
-
-        @pl.when(jnp.logical_not(alone))
+        @pl.when(jnp.logical_not(jnp.logical_and(k == light, own_part)))
         def _():
             pltpu.make_async_remote_copy(
-                leaving.at[k], to, plane_sem.at[0], plane_sem.at[1],
+                leaving.at[k], place, plane_send, arrived,
                 device_id=device(k, half, height), device_id_type=MESH,
             ).start()
 
@@ -426,16 +477,21 @@
 
     lax.fori_loop(0, SLABS // 2, advance_and_send, carry)
 
+    @pl.when(own_part)
+    def _():
+        pltpu.make_async_copy(leaving.at[light], place, arrived).start()
+
     @pl.loop(BEFORE_MARCH, BLOCKS)
     def _(m):
         shading(m)
 
-    pltpu.make_async_copy(planes, planes, plane_sem.at[1]).wait()
-
+
+    copies = []
     for m in range(BLOCKS):
+        pltpu.make_async_copy(planes.at[m], planes.at[m], plane_recv.at[m]).wait()
         lanes = pl.ds(128 * m, 128)
         for pair in range(2):
-            even, odd = planes[EIGHTHS * pair + 2 * m], planes[EIGHTHS * pair + 2 * m + 1]
+            even, odd = planes[m, pair], planes[m, 2 + pair]
             entering = (
                 jnp.where(lane < 64, even, pltpu.roll(odd, 64, 1)),
                 jnp.where(lane < 64, pltpu.roll(even, 64, 1), odd),
@@ -443,26 +499,34 @@
             for i in range(2):
                 c = 2 * pair + i
                 seen = jnp.sum(shade[c, m] * entering[i][None], axis=1)
-                out[c, :, lanes] = seen * albedo[HALF * depth + c]
-
-    pltpu.make_async_copy(
-        columns.at[pl.ds(0, len(NEAR) + 2 * len(FAR))], columns.at[pl.ds(0, len(NEAR) + 2 * len(FAR))], col_send
-    ).wait()
-    pltpu.make_async_copy(
-        columns.at[pl.ds(0, len(NEAR) + 1)], columns.at[pl.ds(0, len(NEAR) + 1)], relay_sem.at[0]
-    ).wait()
+                image[c, :, lanes] = seen * albedo[HALF * depth + c]
+        copy = pltpu.make_async_copy(image.at[:, :, lanes], out.at[:, :, lanes], out_sem.at[m])
+        copy.start()
+        copies.append(copy)
+
+    wait_blocks(len(NEAR) + 2 * len(FAR), col_send)
+    for n, to in enumerate(ends):
+        away = hops_between(to, light)
+
+        @pl.when(jnp.logical_and(away > 0, away <= 2))
+        def _():
+            wait_blocks(1, late_send.at[n])
+
+    @pl.when(late)
+    def _():
+        wait_blocks(1, relay_sem.at[0])
+
+    @pl.when(jnp.logical_not(late))
+    def _():
+        wait_blocks(len(NEAR) + 1, relay_sem.at[0])
 
     @pl.when(has_above)
     def _():
-        pltpu.make_async_copy(rims, rims, up_send).wait()
+        rim_up.wait_send()
 
     @pl.when(has_below)
     def _():
-        pltpu.make_async_copy(rims, rims, down_send).wait()
-
-    @pl.when(on_edge)
-    def _():
-        share_rims.wait_send()
+        rim_down.wait_send()
 
     share.wait_send()
     share_lamp.wait_send()
@@ -471,26 +535,28 @@
     def _():
         pltpu.make_async_copy(lampedge, lampedge, lampedge_sem.at[0]).wait()
 
-    @pl.when(half == depth)
+    @pl.when(own_part)
     def _():
         part = leaving.at[pl.ds(0, SLABS - 1)]
-        pltpu.make_async_copy(part, part, plane_sem.at[0]).wait()
-
-    @pl.when(half != depth)
-    def _():
-        pltpu.make_async_copy(leaving, leaving, plane_sem.at[0]).wait()
+        pltpu.make_async_copy(part, part, plane_send).wait()
+
+    @pl.when(jnp.logical_not(own_part))
+    def _():
+        pltpu.make_async_copy(leaving, leaving, plane_send).wait()
+
+    for copy in copies:
+        copy.wait()
 
 
 def local(density, active_list, light_dir, lamp_plane, extinction, blur_weights, albedo):
     f32 = jnp.float32
-    vmem = pl.BlockSpec(memory_space=pltpu.VMEM)
     anywhere = pl.BlockSpec(memory_space=pl.ANY)
     dma = pltpu.SemaphoreType.DMA
     return pl.pallas_call(
         body,
         out_shape=jax.ShapeDtypeStruct((HALF, SLICES, WIDTH), f32),
         in_specs=[anywhere] * 7,
-        out_specs=vmem,
+        out_specs=anywhere,
         scratch_shapes=[
             pltpu.VMEM(active_list.shape, jnp.int32),
             pltpu.SMEM(light_dir.shape, jnp.int32),
@@ -502,8 +568,7 @@
             pltpu.VMEM((2, SLICES, ROWS, WIDTH), f32),
             pltpu.VMEM((EIGHTHS, ROWS, 128), f32),
             pltpu.VMEM((2, 8, 128), f32),
-            pltpu.VMEM((2 * SLABS, ROWS, 128), f32),
-            pltpu.VMEM((2, SLABS, 8, 128), f32),
+            pltpu.VMEM((2, 8, 128), f32),
             pltpu.VMEM((2 * SLABS, ROWS, 128), f32),
             pltpu.VMEM((EIGHTHS, HALF, ROWS, 128), f32),
             pltpu.VMEM((2, HALF, 8, 128), f32),
@@ -511,10 +576,13 @@
             pltpu.VMEM((2, 2, 8, 128), f32),
             pltpu.VMEM((2, SLABS, DEPTH, 128), f32),
             pltpu.VMEM((SLABS, DEPTH, 128), f32),
-            pltpu.VMEM((2 * EIGHTHS, DEPTH, 128), f32),
+            pltpu.VMEM((BLOCKS, 4, DEPTH, 128), f32),
             pltpu.VMEM((HALF, BLOCKS, SLICES, DEPTH, 128), f32),
             pltpu.VMEM((2, 25, 8, 128), f32),
-            dma((10,)), dma(()), dma(()), dma(()), dma((2,)), dma(()), dma(()), dma(()), dma((2,)), dma((2,)), dma((2,)), dma((2,)), dma((2,)),
+            pltpu.VMEM((2, DEPTH + 16, 128), f32),
+            pltpu.VMEM((HALF, SLICES, WIDTH), f32),
+            dma((10,)), dma(()), dma((4,)), dma(()), dma(()), dma((2,)), dma((2,)), dma((2,)), dma((2,)), dma((2,)), dma((2,)),
+            dma(()), dma((BLOCKS,)), dma((BLOCKS,)),
         ],
         compiler_params=pltpu.CompilerParams(
             collective_id=0, has_side_effects=True, vmem_limit_bytes=63 * 1024 * 1024

time: 25.5 us -> 25.2 us (0.988)
  the two profiles are of different devices: /device:TPU:99 before, /device:TPU:98 now
where the time goes in v3:
time: 25.2 us; the launch traced here: 24.8 us
  Pallas kernels  23.2 us (92%)
  local copies, waits for them, and re-layouts  1.57 us (6%)
    pallas_call x1, Pallas kernels, local(): pl.pallas_call(body, out_shape=jax.ShapeDtypeStruct((HALF, SLICES, WIDTH)...  23.2 us
    unnamed x1, local copies, waits for them, and re-layouts  1.57 us

profile of v3, /device:TPU:98, one launch (start us, length us, event | category | flops | bytes accessed | tf_op | source)
XLA Modules:
  0.0 24.8 jit_solution(8481002211167947884)
XLA Ops:
  0.0 23.2 %march_and_shade.1 = f32[4,16,512]{2,1,0:T(8,128)} custom-call(f32[16,16,512]{2,1,0:T(8,128)} %density.1, s32[2,384]{1,0:T(2,128)} %active_hbm.1, s32[8]{0:T(128)} %light_dir_hbm.1, f32[8,16,512]{2,1,0:T(8,128)} %lamp.1, f32[8]{0:T(128)} %extinction_hbm.1, f32[8,25]{1,0:T(8,128)} %blur_hbm.1, f32[8]{0:T(128)} %albedo_hbm.1), custom_call_target="tpu_custom_call" | custom-call | tf_op jit(solution)/shard_map/march_and_shade/pallas_call | solution.py:555
  23.2 1.6 %copy.9 = f32[4,16,512]{2,1,0:T(8,128)} copy(f32[4,16,512]{2,1,0:T(8,128)} %march_and_shade.1) | data formatting | bytes 262144

commit v4 on v3

--- a/solution.py
+++ b/solution.py
@@ -112,6 +112,8 @@
         )
         for i in range(4)
     ]
+    load_active = pltpu.make_async_copy(active_hbm, active, load_sem.at[5])
+    load_active.start()
     for load in loads:
         load.start()
     barrier = pltpu.get_barrier_semaphore()
@@ -146,14 +148,12 @@
 
     load_lamp = pltpu.make_async_copy(lamp.at[pl.ds(HALF * half, HALF)], lampv, load_sem.at[4])
     load_lamp.start()
-    load_active = pltpu.make_async_copy(active_hbm, active, load_sem.at[5])
     load_small = [
         pltpu.make_async_copy(light_dir_hbm, light_dir, load_sem.at[6]),
         pltpu.make_async_copy(extinction_hbm, extinction, load_sem.at[7]),
         pltpu.make_async_copy(blur_hbm, blur_weights, load_sem.at[8]),
         pltpu.make_async_copy(albedo_hbm, albedo, load_sem.at[9]),
     ]
-    load_active.start()
     for load in load_small:
         load.start()
 
@@ -282,11 +282,13 @@
 
     ends = [to for to in range(SLABS) if eighth_of(to) in (0, EIGHTHS - 1)]
     for to in ends:
-        away = hops_between(to, light)
-
-        @pl.when(away > 2)
+
+        @pl.when(hops_between(to, light) > 2)
         def _():
             send_far(to)
+
+    for to in ends:
+        away = hops_between(to, light)
 
         @pl.when(jnp.logical_and(away > 0, away <= 2))
         def _():
@@ -487,7 +489,7 @@
 
 
     copies = []
-    for m in range(BLOCKS):
+    for m in (1, 2, 3, 0):
         pltpu.make_async_copy(planes.at[m], planes.at[m], plane_recv.at[m]).wait()
         lanes = pl.ds(128 * m, 128)
         for pair in range(2):

time: 25.2 us -> 24.9 us (0.988); the launches traced: 24.8 us -> 24.8 us
  no operation moved by 1% of the time
where the time goes in v4:
time: 24.9 us; the launch traced here: 24.8 us
  Pallas kernels  23.2 us (93%)
  local copies, waits for them, and re-layouts  1.57 us (6%)
    pallas_call x1, Pallas kernels, local(): pl.pallas_call(body, out_shape=jax.ShapeDtypeStruct((HALF, SLICES, WIDTH)...  23.2 us
    unnamed x1, local copies, waits for them, and re-layouts  1.57 us

profile of v4, /device:TPU:98, one launch (start us, length us, event | category | flops | bytes accessed | tf_op | source)
XLA Modules:
  0.0 24.8 jit_solution(16679995468170317548)
XLA Ops:
  0.0 23.2 %march_and_shade.1 = f32[4,16,512]{2,1,0:T(8,128)} custom-call(f32[16,16,512]{2,1,0:T(8,128)} %density.1, s32[2,384]{1,0:T(2,128)} %active_hbm.1, s32[8]{0:T(128)} %light_dir_hbm.1, f32[8,16,512]{2,1,0:T(8,128)} %lamp.1, f32[8]{0:T(128)} %extinction_hbm.1, f32[8,25]{1,0:T(8,128)} %blur_hbm.1, f32[8]{0:T(128)} %albedo_hbm.1), custom_call_target="tpu_custom_call" | custom-call | tf_op jit(solution)/shard_map/march_and_shade/pallas_call | solution.py:557
  23.2 1.6 %copy.9 = f32[4,16,512]{2,1,0:T(8,128)} copy(f32[4,16,512]{2,1,0:T(8,128)} %march_and_shade.1) | data formatting | bytes 262144

commit v5 on v4

--- a/solution.py
+++ b/solution.py
@@ -16,8 +16,8 @@
 BRICK_ROWS = 8
 EIGHTHS = 8
 HALF = 4
-BEFORE_RELAY = 1
-BEFORE_MARCH = 2
+BEFORE_RELAY = 0
+BEFORE_MARCH = 1
 SIDE = 4
 
 
@@ -121,25 +121,25 @@
     def greet(to, core, at):
         pl.semaphore_signal(barrier, inc=1, device_id=device(to, core, at), device_id_type=MESH)
 
+    @pl.when(has_below)
+    def _():
+        greet(light, depth, below)
+
+    @pl.when(has_above)
+    def _():
+        greet(light, depth, above)
+
+    @pl.when(low_edge)
+    def _():
+        greet(light, sibling, below)
+
+    @pl.when(high_edge)
+    def _():
+        greet(light, sibling, above)
+
     for step in FAR:
         for core in range(2):
             greet(chip_at(light, step), core, height)
-
-    @pl.when(has_below)
-    def _():
-        greet(light, depth, below)
-
-    @pl.when(has_above)
-    def _():
-        greet(light, depth, above)
-
-    @pl.when(low_edge)
-    def _():
-        greet(light, sibling, below)
-
-    @pl.when(high_edge)
-    def _():
-        greet(light, sibling, above)
 
     for step in NEAR:
         for core in range(2):
@@ -450,7 +450,7 @@
             steps[i, s + 1] = plane[i]
         return plane, later
 
-    carry = lax.fori_loop(0, SLABS // 2 - 1, advance, (tuple(start), factors(0)))
+    carry = lax.fori_loop(0, SLABS // 2 - 1, advance, (tuple(start), factors(0)), unroll=True)
 
     own_part = half == depth
     arrived = plane_recv.at[lax.div(eighth, 2)]
@@ -477,7 +477,7 @@
 
         return carry
 
-    lax.fori_loop(0, SLABS // 2, advance_and_send, carry)
+    lax.fori_loop(0, SLABS // 2, advance_and_send, carry, unroll=True)
 
     @pl.when(own_part)
     def _():

time: 24.9 us -> 24.8 us (level)
  no operation moved by 1% of the time
where the time goes in v5:
time: 24.8 us; the launch traced here: 24.6 us
  Pallas kernels  23.1 us (93%)
  local copies, waits for them, and re-layouts  1.57 us (6%)
    pallas_call x1, Pallas kernels, local(): pl.pallas_call(body, out_shape=jax.ShapeDtypeStruct((HALF, SLICES, WIDTH)...  23.1 us
    unnamed x1, local copies, waits for them, and re-layouts  1.57 us

profile of v5, /device:TPU:98, one launch (start us, length us, event | category | flops | bytes accessed | tf_op | source)
XLA Modules:
  0.0 24.6 jit_solution(17577217792672390981)
XLA Ops:
  0.0 23.1 %march_and_shade.1 = f32[4,16,512]{2,1,0:T(8,128)} custom-call(f32[16,16,512]{2,1,0:T(8,128)} %density.1, s32[2,384]{1,0:T(2,128)} %active_hbm.1, s32[8]{0:T(128)} %light_dir_hbm.1, f32[8,16,512]{2,1,0:T(8,128)} %lamp.1, f32[8]{0:T(128)} %extinction_hbm.1, f32[8,25]{1,0:T(8,128)} %blur_hbm.1, f32[8]{0:T(128)} %albedo_hbm.1), custom_call_target="tpu_custom_call" | custom-call | tf_op jit(solution)/shard_map/march_and_shade/pallas_call | solution.py:557
  23.1 1.6 %copy.9 = f32[4,16,512]{2,1,0:T(8,128)} copy(f32[4,16,512]{2,1,0:T(8,128)} %march_and_shade.1) | data formatting | bytes 262144

commit v6 on v5

--- a/solution.py
+++ b/solution.py
@@ -471,13 +471,24 @@
         early = [steps[i, SLABS - 2 - s] for i in range(2)]
         front = [jnp.where(down[i], early[i], late[i]) for i in range(2)]
         rear = [jnp.where(down[i], late[i], early[i]) for i in range(2)]
-        for k, pair in ((s + 1, front), (SLABS - 2 - s, rear)):
+        for k, pair in ((SLABS - 2 - s, rear), (s + 1, front)):
             leaving[k] = jnp.where(lane < 64, pltpu.roll(pair[0], 96, 1), pltpu.roll(pair[1], 32, 1))
-            send(k)
+
+            @pl.when(hops_between(k, light) > 1)
+            def _():
+                send(k)
 
         return carry
 
     lax.fori_loop(0, SLABS // 2, advance_and_send, carry, unroll=True)
+
+    for step in OTHERS[::-1]:
+        if hops(*step) == 1:
+            send(chip_at(light, step))
+
+    @pl.when(jnp.logical_not(own_part))
+    def _():
+        send(light)
 
     @pl.when(own_part)
     def _():

time: 24.8 us -> 24.4 us (0.984)
  Pallas kernels: 23.1 us -> 22.7 us
    pallas_call x1, Pallas kernels: 23.1 us -> 22.7 us  [local(): pl.pallas_call(body, out_shape=jax.ShapeDtypeStruct((HALF, SLICES, WIDTH)...]
where the time goes in v6:
time: 24.4 us; the launch traced here: 24.3 us
  Pallas kernels  22.7 us (93%)
  local copies, waits for them, and re-layouts  1.57 us (6%)
    pallas_call x1, Pallas kernels, local(): pl.pallas_call(body, out_shape=jax.ShapeDtypeStruct((HALF, SLICES, WIDTH)...  22.7 us
    unnamed x1, local copies, waits for them, and re-layouts  1.57 us

profile of v6, /device:TPU:98, one launch (start us, length us, event | category | flops | bytes accessed | tf_op | source)
XLA Modules:
  0.0 24.3 jit_solution(6831510051977629776)
XLA Ops:
  0.0 22.7 %march_and_shade.1 = f32[4,16,512]{2,1,0:T(8,128)} custom-call(f32[16,16,512]{2,1,0:T(8,128)} %density.1, s32[2,384]{1,0:T(2,128)} %active_hbm.1, s32[8]{0:T(128)} %light_dir_hbm.1, f32[8,16,512]{2,1,0:T(8,128)} %lamp.1, f32[8]{0:T(128)} %extinction_hbm.1, f32[8,25]{1,0:T(8,128)} %blur_hbm.1, f32[8]{0:T(128)} %albedo_hbm.1), custom_call_target="tpu_custom_call" | custom-call | tf_op jit(solution)/shard_map/march_and_shade/pallas_call | solution.py:568
  22.7 1.6 %copy.9 = f32[4,16,512]{2,1,0:T(8,128)} copy(f32[4,16,512]{2,1,0:T(8,128)} %march_and_shade.1) | data formatting | bytes 262144

commit v7 on v6

--- a/solution.py
+++ b/solution.py
@@ -27,7 +27,7 @@
 
 OTHERS = sorted(
     ((down, right) for down in range(SIDE) for right in range(SIDE) if down or right),
-    key=lambda step: -hops(*step),
+    key=lambda step: (-hops(*step), -(step[0] == 2) - (step[1] == 2)),
 )
 FAR = [step for step in OTHERS if hops(*step) > 2]
 NEAR = [step for step in OTHERS if hops(*step) <= 2]

time: 24.4 us -> 24.4 us (level)
  no operation moved by 1% of the time
where the time goes in v7:
time: 24.4 us; the launch traced here: 24.3 us
  Pallas kernels  22.7 us (93%)
  local copies, waits for them, and re-layouts  1.57 us (6%)
    pallas_call x1, Pallas kernels, local(): pl.pallas_call(body, out_shape=jax.ShapeDtypeStruct((HALF, SLICES, WIDTH)...  22.7 us
    unnamed x1, local copies, waits for them, and re-layouts  1.57 us

profile of v7, /device:TPU:98, one launch (start us, length us, event | category | flops | bytes accessed | tf_op | source)
XLA Modules:
  0.0 24.3 jit_solution(13469741689509925435)
XLA Ops:
  0.0 22.7 %march_and_shade.1 = f32[4,16,512]{2,1,0:T(8,128)} custom-call(f32[16,16,512]{2,1,0:T(8,128)} %density.1, s32[2,384]{1,0:T(2,128)} %active_hbm.1, s32[8]{0:T(128)} %light_dir_hbm.1, f32[8,16,512]{2,1,0:T(8,128)} %lamp.1, f32[8]{0:T(128)} %extinction_hbm.1, f32[8,25]{1,0:T(8,128)} %blur_hbm.1, f32[8]{0:T(128)} %albedo_hbm.1), custom_call_target="tpu_custom_call" | custom-call | tf_op jit(solution)/shard_map/march_and_shade/pallas_call | solution.py:568
  22.7 1.6 %copy.9 = f32[4,16,512]{2,1,0:T(8,128)} copy(f32[4,16,512]{2,1,0:T(8,128)} %march_and_shade.1) | data formatting | bytes 262144
